TPU v7x, 32 devices: a whole 2x2x4 slice. The times are simulated.
32 devices in a mesh: ep: 4 (over y, core), dp: 8 (over z, x).
Axes of the slice: x: 2, y: 2, z: 4, core: 2. Of those that a mesh axis runs over, the one named last changes fastest.
Arguments:
- fwd_tokens: bfloat16 [512, 2048], P(('ep', 'dp')), may hold values from -6 to 6
- fwd_routes: int32 [512, 2], P(('ep', 'dp')), may hold values from 0 to 3, as said below
- fwd_weights: float32 [512, 2], P(('ep', 'dp')), may hold values from 0.05 to 0.4
- bwd_grads: bfloat16 [512, 2048], P(('ep', 'dp')), may hold values from -6 to 6
- bwd_routes: int32 [512, 2], P(('ep', 'dp')), may hold values from 0 to 3, as said below
- bwd_weights: float32 [512, 2], P(('ep', 'dp')), may hold values from 0.05 to 0.4
- bwd_saved: bfloat16 [4, 256, 2048], P('ep', 'dp'), may hold values from -6 to 6
- w_gate: bfloat16 [4, 2048, 384], P('ep'), may hold values from -0.125 to 0.125
- w_up: bfloat16 [4, 2048, 384], P('ep'), may hold values from -0.125 to 0.125
- w_down: bfloat16 [4, 384, 2048], P('ep'), may hold values from -0.3125 to 0.3125
Outputs:
- fwd_out: bfloat16 [512, 2048], P(('ep', 'dp'))
- bwd_input_grad: bfloat16 [512, 2048], P(('ep', 'dp'))
- down_grad: float32 [4, 2048, 384], P('ep', 'dp')
Inputs may be any that keep to these rules, and one draw needn't show every extreme that they name: `fwd_routes`: each token names 2 different experts, and the 16 tokens of each aligned block (one device's tokens) name every expert exactly 8 times. `bwd_routes`: each token names 2 different experts, and the 16 tokens of each aligned block (one device's tokens) name every expert exactly 8 times.
All inputs are finite; a program needn't handle non-finite values.
Results may differ from a plain program's by a relative error of at most 0.0064.
Values may be sent and summed in bfloat16 or wider, within the bound.
A program may use at most 64 MiB of HBM per device.

v0:
```python
import jax
import jax.numpy as jnp
from jax import lax
from jax.sharding import PartitionSpec as P


def slot_tables(routes, weights, experts):
    token_count, picks = routes.shape
    slot_count = token_count * picks // experts
    hits = routes[:, :, None] == jnp.arange(experts, dtype=jnp.int32)[None, None, :]
    member = jnp.sum(hits.astype(jnp.int32), axis=1)
    before = jnp.cumsum(member, axis=0) - member
    slot_ids = jnp.arange(slot_count, dtype=jnp.int32)[None, :, None]
    chosen = (member.T[:, None, :] == 1) & (before.T[:, None, :] == slot_ids)
    mixing = jnp.sum(jnp.where(hits, weights[:, :, None], 0.0), axis=1)
    return (chosen, mixing)


def expert_forward(arrived, w_gate, w_up, w_down):
    sources, local_experts, slot_count, model_width = arrived.shape
    rows_in = arrived[:, 0].reshape(sources * slot_count, model_width)
    gate_pre = jnp.dot(rows_in, w_gate[0], preferred_element_type=jnp.float32)
    up_pre = jnp.dot(rows_in, w_up[0], preferred_element_type=jnp.float32)
    hidden = (jax.nn.silu(gate_pre) * up_pre).astype(jnp.bfloat16)
    expert_out = jnp.dot(hidden, w_down[0], preferred_element_type=jnp.float32).astype(jnp.bfloat16)
    results = [expert_out.reshape(sources, slot_count, model_width)]
    return jnp.stack(results, axis=1)


def expert_backward(cotangent, bwd_saved, w_gate, w_up, w_down):
    sources, local_experts, slot_count, model_width = cotangent.shape
    contract_last = (((1,), (1,)), ((), ()))
    cot_rows = cotangent[:, 0].reshape(sources * slot_count, model_width)
    saved_rows = bwd_saved[0]
    gate_pre = jnp.dot(saved_rows, w_gate[0], preferred_element_type=jnp.float32)
    up_pre = jnp.dot(saved_rows, w_up[0], preferred_element_type=jnp.float32)
    sigma = jax.nn.sigmoid(gate_pre)
    hidden = (gate_pre * sigma * up_pre).astype(jnp.bfloat16)
    dact = lax.dot_general(cot_rows, w_down[0], contract_last, preferred_element_type=jnp.float32)
    dgate = (dact * up_pre * sigma * (1.0 + gate_pre * (1.0 - sigma))).astype(jnp.bfloat16)
    dup_rows = (dact * gate_pre * sigma).astype(jnp.bfloat16)
    row_grad = lax.dot_general(dgate, w_gate[0], contract_last, preferred_element_type=jnp.float32)
    row_grad = row_grad + lax.dot_general(
        dup_rows, w_up[0], contract_last, preferred_element_type=jnp.float32
    )
    row_grads = [row_grad.astype(jnp.bfloat16).reshape(sources, slot_count, model_width)]
    cot_list = [cot_rows]
    hidden_list = [hidden]
    return (
        jnp.stack(row_grads, axis=1),
        jnp.stack(cot_list, axis=0),
        jnp.stack(hidden_list, axis=0),
    )


def weight_terms(cot_all, hidden_all):
    return jnp.einsum("ern,erf->enf", cot_all, hidden_all, preferred_element_type=jnp.float32)


def on_device(
    fwd_tokens,
    fwd_routes,
    fwd_weights,
    bwd_grads,
    bwd_routes,
    bwd_weights,
    bwd_saved,
    w_gate,
    w_up,
    w_down,
):
    groups = lax.axis_size("ep")
    local_experts = w_gate.shape[0]
    experts = groups * local_experts
    model_width = fwd_tokens.shape[1]
    fwd_chosen, fwd_mixing = slot_tables(fwd_routes, fwd_weights, experts)
    bwd_chosen, bwd_mixing = slot_tables(bwd_routes, bwd_weights, experts)
    slot_count = fwd_chosen.shape[1]
    layout = (groups, local_experts, slot_count, model_width)
    fwd_select = fwd_chosen.astype(jnp.bfloat16)
    bwd_select = bwd_chosen.astype(jnp.bfloat16)
    send_tokens = jnp.einsum(
        "est,td->esd", fwd_select, fwd_tokens, preferred_element_type=jnp.float32
    )
    send_tokens = send_tokens.astype(jnp.bfloat16).reshape(layout)
    bwd_scale = jnp.sum(jnp.where(bwd_chosen, bwd_mixing.T[:, None, :], 0.0), axis=2)
    picked_grads = jnp.einsum(
        "est,td->esd", bwd_select, bwd_grads, preferred_element_type=jnp.float32
    )
    send_grads = (picked_grads * bwd_scale[:, :, None]).astype(jnp.bfloat16).reshape(layout)
    arrived = lax.all_to_all(send_tokens, "ep", split_axis=0, concat_axis=0, tiled=True)
    expert_out = expert_forward(arrived, w_gate, w_up, w_down)
    returned = lax.all_to_all(expert_out, "ep", split_axis=0, concat_axis=0, tiled=True)
    returned = returned.reshape(experts, slot_count, model_width)
    per_expert = jnp.einsum(
        "est,esd->etd", fwd_select, returned, preferred_element_type=jnp.float32
    )
    combined = jnp.sum(fwd_mixing.T[:, :, None] * per_expert, axis=0)
    fwd_out = combined.astype(jnp.bfloat16)
    arrived = lax.all_to_all(send_grads, "ep", split_axis=0, concat_axis=0, tiled=True)
    row_grads, cot_all, hidden_all = expert_backward(arrived, bwd_saved, w_gate, w_up, w_down)
    home_rows = lax.all_to_all(row_grads, "ep", split_axis=0, concat_axis=0, tiled=True)
    down_grad = lax.psum_scatter(
        weight_terms(cot_all, hidden_all), "dp", scatter_dimension=1, tiled=True
    )
    home_rows = home_rows.reshape(experts, slot_count, model_width)
    input_grad = jnp.einsum(
        "est,esd->td", bwd_select, home_rows, preferred_element_type=jnp.float32
    )
    bwd_input_grad, down_grad = (input_grad.astype(jnp.bfloat16), down_grad)
    return (fwd_out, bwd_input_grad, down_grad)


def solution(mesh):
    in_specs = (
        P(("ep", "dp"), None),
        P(("ep", "dp"), None),
        P(("ep", "dp"), None),
        P(("ep", "dp"), None),
        P(("ep", "dp"), None),
        P(("ep", "dp"), None),
        P("ep", "dp", None),
        P("ep", None, None),
        P("ep", None, None),
        P("ep", None, None),
    )
    out_specs = (P(("ep", "dp"), None), P(("ep", "dp"), None), P("ep", "dp", None))
    return jax.shard_map(
        on_device, mesh=mesh, in_specs=in_specs, out_specs=out_specs, check_vma=False
    )
```

profile of v0, /device:TPU:0, one launch (start us, length us, event | category | flops | bytes accessed | tf_op | source)
XLA Modules:
  0.0 103.9 jit_solution(3698571487600351875)
XLA Ops:
  7.2 0.8 convert_reduce_fusion
  8.0 0.1 copy.38
  8.1 0.7 select_reduce_fusion.1
  8.9 0.1 copy.40
  8.9 0.1 select_reduce_fusion
  9.0 1.7 %fusion.5 = bf16[4,1,8,2048]{3,2,1,0:T(8,128)(2,1)} fusion(f32[4,8]{1,0:T(4,128)S(1)} %select_reduce_fusion, bf16[16,2048]{1,0:T(8,128)(2,1)} %param.13, s32[4,16]{1,0:T(4,128)S(1)} %copy.40, pred[4,16]{1,0:T(4,128)(4,1)S(1)} %compare_bitcast_fusion), kind=kOutput, calls=%fused_computation.11 | convolution fusion | flops 2229248 | bytes 197056 | tf_op jit(solution)/shard_map/est,td->esd/dot_general | solution.py:87
  10.7 4.2 %all-to-all-start.2 = ((bf16[4,1,8,2048]{3,2,1,0:T(8,128)(2,1)}), bf16[4,1,8,2048]{3,2,1,0:T(8,128)(2,1)S(1)}, u32[]{:S(2)}, u32[]{:S(2)}) async-start(bf16[4,1,8,2048]{3,2,1,0:T(8,128)(2,1)} %fusion.5), calls=%async_computation.2 | async-start | bytes 262144 | tf_op jit(solution)/shard_map/all_to_all | solution.py:100
  14.9 1.8 %fusion.17 = f32[32,384]{1,0:T(8,128)S(1)} fusion(bf16[1,2048,384]{2,1,0:T(8,128)(2,1)} %param.17, bf16[1,32,2048]{2,1,0:T(8,128)(2,1)} %param.16), kind=kOutput, calls=%fused_computation.24 | convolution fusion | flops 50331648 | bytes 1753088 | tf_op jit(solution)/shard_map/dot_general | solution.py:35
  16.8 0.3 fusion.11
  17.1 2.4 %all-to-all-done.2 = bf16[4,1,8,2048]{3,2,1,0:T(8,128)(2,1)S(1)} async-done(((bf16[4,1,8,2048]{3,2,1,0:T(8,128)(2,1)}), bf16[4,1,8,2048]{3,2,1,0:T(8,128)(2,1)S(1)}, u32[]{:S(2)}, u32[]{:S(2)}) %all-to-all-start.2) | async-done | bytes 131104 | tf_op jit(solution)/shard_map/all_to_all | solution.py:100
  19.6 2.3 %convolution_bitcast_fusion = f32[1,2048,384]{2,1,0:T(8,128)} fusion(bf16[4,1,8,2048]{3,2,1,0:T(8,128)(2,1)S(1)} %all-to-all-done.2, f32[32,384]{1,0:T(8,128)S(1)} %fusion.11, f32[32,384]{1,0:T(8,128)S(1)} %fusion.17), kind=kOutput, calls=%fused_computation | convolution fusion | flops 50405376 | bytes 3375104 | tf_op jit(solution)/shard_map/ern,erf->enf/dot_general | solution.py:57
  21.9 0.0 reduce-scatter.2.cloned.1.call-update
  21.9 0.6 copy-done.10
  22.5 0.1 copy.33
  22.7 0.1 copy.35
  22.8 0.8 fusion.2
  23.6 3.3 %all-to-all-start = ((bf16[4,1,8,2048]{3,2,1,0:T(8,128)(2,1)}), bf16[4,1,8,2048]{3,2,1,0:T(8,128)(2,1)S(1)}, u32[]{:S(2)}, u32[]{:S(2)}) async-start(bf16[4,1,8,2048]{3,2,1,0:T(8,128)(2,1)} %fusion.2), calls=%async_computation | async-start | bytes 262144 | tf_op jit(solution)/shard_map/all_to_all | solution.py:91
  26.9 0.6 select_reduce_fusion.2
  27.5 4.0 %all-to-all-done = bf16[4,1,8,2048]{3,2,1,0:T(8,128)(2,1)S(1)} async-done(((bf16[4,1,8,2048]{3,2,1,0:T(8,128)(2,1)}), bf16[4,1,8,2048]{3,2,1,0:T(8,128)(2,1)S(1)}, u32[]{:S(2)}, u32[]{:S(2)}) %all-to-all-start) | async-done | bytes 131104 | tf_op jit(solution)/shard_map/all_to_all | solution.py:91
  31.5 0.3 fusion.19
  31.9 2.8 %fusion.3 = bf16[4,1,8,2048]{3,2,1,0:T(8,128)(2,1)} fusion(bf16[1,384,2048]{2,1,0:T(8,128)(2,1)} %param.19, bf16[1,2048,384]{2,1,0:T(8,128)(2,1)S(1)} %copy-done, bf16[4,1,8,2048]{3,2,1,0:T(8,128)(2,1)S(1)} %all-to-all-done, f32[32,384]{1,0:T(8,128)S(1)} %fusion.19), kind=kOutput, calls=%fused_computation.9 | convolution fusion | flops 100802560 | bytes 3457024 | tf_op jit(solution)/shard_map/dot_general | solution.py:25
  34.7 3.9 %all-to-all-start.1 = ((bf16[4,1,8,2048]{3,2,1,0:T(8,128)(2,1)}), bf16[4,1,8,2048]{3,2,1,0:T(8,128)(2,1)}, u32[]{:S(2)}, u32[]{:S(2)}) async-start(bf16[4,1,8,2048]{3,2,1,0:T(8,128)(2,1)} %fusion.3), calls=%async_computation.1 | async-start | bytes 262144 | tf_op jit(solution)/shard_map/all_to_all | solution.py:93
  38.6 2.0 %fusion.7 = f32[32,384]{1,0:T(8,128)S(1)} fusion(bf16[1,384,2048]{2,1,0:T(8,128)(2,1)} %param.19, bf16[4,1,8,2048]{3,2,1,0:T(8,128)(2,1)S(1)} %all-to-all-done.2), kind=kOutput, calls=%fused_computation.14 | convolution fusion | flops 50331648 | bytes 1753088 | tf_op jit(solution)/shard_map/dot_general | solution.py:39
  40.6 0.6 fusion.15
  41.2 0.0 copy-start.12
  41.3 1.2 %fusion.4 = bf16[4,1,8,2048]{3,2,1,0:T(8,128)(2,1)} fusion(f32[32,2048]{1,0:T(8,128)S(1)} %fusion.15, bf16[1,2048,384]{2,1,0:T(8,128)(2,1)S(1)} %copy-done, f32[32,384]{1,0:T(8,128)S(1)} %fusion.7, f32[32,384]{1,0:T(8,128)S(1)} %fusion.17), kind=kOutput, calls=%fused_computation.10 | convolution fusion | flops 50536448 | bytes 2064384 | tf_op jit(solution)/shard_map/dot_general | solution.py:43
  42.5 0.8 all-to-all-done.1
  43.3 3.3 %all-to-all-start.3 = ((bf16[4,1,8,2048]{3,2,1,0:T(8,128)(2,1)}), bf16[4,1,8,2048]{3,2,1,0:T(8,128)(2,1)S(1)}, u32[]{:S(2)}, u32[]{:S(2)}) async-start(bf16[4,1,8,2048]{3,2,1,0:T(8,128)(2,1)} %fusion.4), calls=%async_computation.3 | async-start | bytes 262144 | tf_op jit(solution)/shard_map/all_to_all | solution.py:102
  46.7 1.9 %fusion.21 = bf16[16,2048]{1,0:T(8,128)(2,1)} fusion(f32[4,16]{1,0:T(4,128)S(1)} %bitcast.86, bf16[4,1,8,2048]{3,2,1,0:T(8,128)(2,1)} %all-to-all-done.1, s32[4,16]{1,0:T(4,128)S(1)} %copy-done.7, pred[4,16]{1,0:T(4,128)(4,1)S(1)} %copy-done.12), kind=kOutput, calls=%fused_computation.28 | convolution fusion | flops 2327552 | bytes 197184 | tf_op jit(solution)/shard_map/est,esd->etd/dot_general | solution.py:95
  48.6 2.7 %all-to-all-done.3 = bf16[4,1,8,2048]{3,2,1,0:T(8,128)(2,1)S(1)} async-done(((bf16[4,1,8,2048]{3,2,1,0:T(8,128)(2,1)}), bf16[4,1,8,2048]{3,2,1,0:T(8,128)(2,1)S(1)}, u32[]{:S(2)}, u32[]{:S(2)}) %all-to-all-start.3) | async-done | bytes 131104 | tf_op jit(solution)/shard_map/all_to_all | solution.py:102
  51.3 0.8 fusion.6
  52.1 44.9 %reduce-scatter.2.cloned.1.call-done = f32[1,256,384]{2,1,0:T(8,128)} async-done(((f32[1,2048,384]{2,1,0:T(8,128)}), f32[1,256,384]{2,1,0:T(8,128)}) %reduce-scatter.2.cloned.1.call-update) | async-done | bytes 393232 | tf_op jit(solution)/shard_map/reduce_scatter | solution.py:103
  (36 shorter events, 0.2 us)
Async XLA Ops:
  7.2 9.6 %copy-start = (bf16[1,2048,384]{2,1,0:T(8,128)(2,1)S(1)}, bf16[1,2048,384]{2,1,0:T(8,128)(2,1)}, u32[]{:S(2)}) copy-start(bf16[1,2048,384]{2,1,0:T(8,128)(2,1)} %param.18) | copy-start | bytes 4718596
  7.2 9.6 %copy-start.2 = (bf16[1,32,2048]{2,1,0:T(8,128)(2,1)S(1)}, bf16[1,32,2048]{2,1,0:T(8,128)(2,1)}, u32[]{:S(2)}) copy-start(bf16[1,32,2048]{2,1,0:T(8,128)(2,1)} %param.16) | copy-start | bytes 393220
  8.0 2.7 %copy-start.8 = (pred[4,16]{1,0:T(4,128)(4,1)}, pred[4,16]{1,0:T(4,128)(4,1)S(1)}, u32[]{:S(2)}) copy-start(pred[4,16]{1,0:T(4,128)(4,1)S(1)} %compare_bitcast_fusion) | copy-start | bytes 196
  8.9 1.8 %copy-start.4 = (s32[4,16]{1,0:T(4,128)}, s32[4,16]{1,0:T(4,128)S(1)}, u32[]{:S(2)}) copy-start(s32[4,16]{1,0:T(4,128)S(1)} %copy.40) | copy-start | bytes 772
  10.7 8.9 %all-to-all-start.2 = ((bf16[4,1,8,2048]{3,2,1,0:T(8,128)(2,1)}), bf16[4,1,8,2048]{3,2,1,0:T(8,128)(2,1)S(1)}, u32[]{:S(2)}, u32[]{:S(2)}) async-start(bf16[4,1,8,2048]{3,2,1,0:T(8,128)(2,1)} %fusion.5), calls=%async_computation.2 | async-start | bytes 262144 | tf_op jit(solution)/shard_map/all_to_all | solution.py:100
  14.9 82.1 %reduce-scatter.2.cloned.1.call-start = ((), (), s32[]{:S(2)}) async-start(), calls=%async_computation.5 | async-start | bytes 3538944 | tf_op jit(solution)/shard_map/reduce_scatter | solution.py:103
  21.8 0.7 copy-start.10
  21.8 0.9 copy-start.3
  21.9 5.1 %copy-start.14 = (f32[16,2]{0,1:T(2,128)S(1)}, f32[16,2]{0,1:T(2,128)}, u32[]{:S(2)}) copy-start(f32[16,2]{0,1:T(2,128)} %param.12) | copy-start | bytes 388
  21.9 9.7 %copy-start.1 = (bf16[1,2048,384]{2,1,0:T(8,128)(2,1)S(1)}, bf16[1,2048,384]{2,1,0:T(8,128)(2,1)}, u32[]{:S(2)}) copy-start(bf16[1,2048,384]{2,1,0:T(8,128)(2,1)} %param.17) | copy-start | bytes 4718596
  22.8 0.8 copy-start.6
  22.8 0.8 copy-start.11
  23.6 7.9 %all-to-all-start = ((bf16[4,1,8,2048]{3,2,1,0:T(8,128)(2,1)}), bf16[4,1,8,2048]{3,2,1,0:T(8,128)(2,1)S(1)}, u32[]{:S(2)}, u32[]{:S(2)}) async-start(bf16[4,1,8,2048]{3,2,1,0:T(8,128)(2,1)} %fusion.2), calls=%async_computation | async-start | bytes 262144 | tf_op jit(solution)/shard_map/all_to_all | solution.py:91
  34.7 8.6 %all-to-all-start.1 = ((bf16[4,1,8,2048]{3,2,1,0:T(8,128)(2,1)}), bf16[4,1,8,2048]{3,2,1,0:T(8,128)(2,1)}, u32[]{:S(2)}, u32[]{:S(2)}) async-start(bf16[4,1,8,2048]{3,2,1,0:T(8,128)(2,1)} %fusion.3), calls=%async_computation.1 | async-start | bytes 262144 | tf_op jit(solution)/shard_map/all_to_all | solution.py:93
  41.2 5.5 %copy-start.7 = (s32[4,16]{1,0:T(4,128)S(1)}, s32[4,16]{1,0:T(4,128)}, u32[]{:S(2)}) copy-start(s32[4,16]{1,0:T(4,128)} %copy-done.6) | copy-start | bytes 772
  41.2 5.5 %copy-start.12 = (pred[4,16]{1,0:T(4,128)(4,1)S(1)}, pred[4,16]{1,0:T(4,128)(4,1)}, u32[]{:S(2)}) copy-start(pred[4,16]{1,0:T(4,128)(4,1)} %copy-done.11) | copy-start | bytes 196
  41.2 5.5 %copy-start.13 = (f32[16,4]{0,1:T(4,128)S(1)}, f32[16,4]{0,1:T(4,128)}, u32[]{:S(2)}) copy-start(f32[16,4]{0,1:T(4,128)} %select_reduce_fusion.2) | copy-start | bytes 772
  41.2 10.0 %copy-start.5 = (s32[4,16]{1,0:T(4,128)S(1)}, s32[4,16]{1,0:T(4,128)}, u32[]{:S(2)}) copy-start(s32[4,16]{1,0:T(4,128)} %copy-done.4) | copy-start | bytes 772
  41.3 10.0 %copy-start.9 = (pred[4,16]{1,0:T(4,128)(4,1)S(1)}, pred[4,16]{1,0:T(4,128)(4,1)}, u32[]{:S(2)}) copy-start(pred[4,16]{1,0:T(4,128)(4,1)} %copy-done.8) | copy-start | bytes 196
  43.3 7.9 %all-to-all-start.3 = ((bf16[4,1,8,2048]{3,2,1,0:T(8,128)(2,1)}), bf16[4,1,8,2048]{3,2,1,0:T(8,128)(2,1)S(1)}, u32[]{:S(2)}, u32[]{:S(2)}) async-start(bf16[4,1,8,2048]{3,2,1,0:T(8,128)(2,1)} %fusion.4), calls=%async_computation.3 | async-start | bytes 262144 | tf_op jit(solution)/shard_map/all_to_all | solution.py:102
Sparse Core Ops, SparseCore 0:
  22.0 75.0 reduce-scatter.1
where the time goes:
time: 105 us; the launch traced here: 104 us
  waiting for transfers between devices  55 us (52%)
  matrix products  16.6 us (16%)
  starting transfers between devices  14.8 us (14%)
  between operations  14.2 us (14%)
  other arithmetic  2.31 us (2%)
  local copies, waits for them, and re-layouts  1.06 us (1%)
    reduce_scatter x1, waiting for transfers between devices, on_device(): lax.psum_scatter(weight_terms(cot_all, hidden_all), 'dp', scatter_dimensi...  44.9 us
    all_to_all x1, starting transfers between devices, on_device(): lax.all_to_all(send_grads, 'ep', split_axis=0, concat_axis=0, tiled=True)  4.24 us
    all_to_all x1, waiting for transfers between devices, on_device(): lax.all_to_all(send_tokens, 'ep', split_axis=0, concat_axis=0, tiled=True)  4 us
    all_to_all x1, starting transfers between devices, on_device(): lax.all_to_all(expert_out, 'ep', split_axis=0, concat_axis=0, tiled=True)  3.94 us
    all_to_all x1, starting transfers between devices, on_device(): lax.all_to_all(row_grads, 'ep', split_axis=0, concat_axis=0, tiled=True)  3.33 us
    all_to_all x1, starting transfers between devices, on_device(): lax.all_to_all(send_tokens, 'ep', split_axis=0, concat_axis=0, tiled=True)  3.32 us
    dot_general x1, matrix products, expert_forward(): jnp.dot(hidden, w_down[0], preferred_element_type=jnp.float32)  2.84 us
    all_to_all x1, waiting for transfers between devices, on_device(): lax.all_to_all(row_grads, 'ep', split_axis=0, concat_axis=0, tiled=True)  2.72 us
  transfers between devices with their start and end apart: 5, of which 5 were waited for; matrix products, arithmetic and copies ran while one was open for 13% of the time, Pallas kernels for 0%

commit v1 on v0

v1 whole, which is shorter than its diff:
```python
import functools

import jax
import jax.numpy as jnp
from jax import lax
from jax.experimental import pallas as pl
from jax.experimental.pallas import tpu as pltpu
from jax.sharding import PartitionSpec as P

BF16, F32 = jnp.bfloat16, jnp.float32
LAST = (((1,), (1,)), ((), ()))
FIRST = (((0,), (0,)), ((), ()))


def matmul(a, b, dims=(((1,), (0,)), ((), ()))):
    return lax.dot_general(a, b, dims, preferred_element_type=F32)


def kernel(
    experts, groups, slots,
    tok_hbm, routes_a_hbm, mix_a_hbm, grad_hbm, routes_b_hbm, mix_b_hbm, saved_hbm, gate_hbm, up_hbm, down_hbm,
    out_a, out_b, out_w,
    tok, routes_a, mix_a, grad, routes_b, mix_b, saved, wgu, wd,
    send_a, send_b, got_a, got_b, ret_a, ret_b, home_a, home_b,
    cols, cols_all, act_all,
    load_sem, ep_send, ep_recv, dp_send, dp_recv,
):
    ep, dp = lax.axis_index("ep"), lax.axis_index("dp")
    width, ff = tok.shape[1], wd.shape[0]
    half = width // 2
    rows = experts * slots

    loads = []
    for src, dst in (
        (routes_b_hbm, routes_b), (mix_b_hbm, mix_b), (grad_hbm, grad),
        (routes_a_hbm, routes_a), (mix_a_hbm, mix_a), (tok_hbm, tok),
        (saved_hbm.at[0], saved),
        (gate_hbm.at[0], wgu.at[:, pl.ds(0, ff)]), (up_hbm.at[0], wgu.at[:, pl.ds(ff, ff)]),
        (down_hbm.at[0], wd),
    ):
        copy = pltpu.make_async_copy(src, dst, load_sem.at[len(loads)])
        copy.start()
        loads.append(copy)

    barrier = pltpu.get_barrier_semaphore()
    for k in range(1, experts):
        pl.semaphore_signal(barrier, inc=1, device_id={"ep": lax.rem(ep + k, experts)}, device_id_type=pl.DeviceIdType.MESH)
    for k in range(1, groups):
        pl.semaphore_signal(barrier, inc=1, device_id={"dp": lax.rem(dp + k, groups)}, device_id_type=pl.DeviceIdType.MESH)

    def exchange(which, src, dst):
        copies = []
        for k in range(1, experts):
            peer = lax.rem(ep + k, experts)
            copy = pltpu.make_async_remote_copy(
                src_ref=src.at[peer], dst_ref=dst.at[ep], send_sem=ep_send.at[which, k], recv_sem=ep_recv.at[which, k],
                device_id={"ep": peer}, device_id_type=pl.DeviceIdType.MESH,
            )
            copy.start()
            copies.append(copy)
        dst[ep] = src[ep]
        return copies

    def spread(which, src_of, dst):
        copies = []
        for k in range(1, groups):
            peer = lax.rem(dp + k, groups)
            copy = pltpu.make_async_remote_copy(
                src_ref=src_of(peer), dst_ref=dst.at[dp], send_sem=dp_send.at[which, k], recv_sem=dp_recv.at[which, k],
                device_id={"dp": peer}, device_id_type=pl.DeviceIdType.MESH,
            )
            copy.start()
            copies.append(copy)
        return copies

    def table(routes, mix):
        top, tokens = routes.shape
        shape = (2 * rows, tokens)
        index = lax.broadcasted_iota(jnp.int32, shape, 0)
        expert = index // (2 * slots)
        slot = (index % slots).astype(F32)
        hit = jnp.zeros(shape, F32)
        weight = jnp.zeros(shape, F32)
        for k in range(top):
            same = routes[pl.ds(k, 1), :] == expert
            hit = jnp.where(same, 1.0, hit)
            weight = weight + jnp.where(same, mix[pl.ds(k, 1), :], 0.0)
        square = (tokens, tokens)
        earlier = lax.broadcasted_iota(jnp.int32, square, 0) < lax.broadcasted_iota(jnp.int32, square, 1)
        before = matmul(hit.astype(BF16), jnp.where(earlier, 1.0, 0.0).astype(BF16))
        chosen = jnp.where(before == slot, hit, 0.0)
        part = (index // slots) % 2
        halves = [jnp.where(part == h, chosen, 0.0) for h in range(2)]
        return halves, chosen * weight, weight

    def pick(halves, source):
        return matmul(halves[0].astype(BF16), source[:, :half]) + matmul(halves[1].astype(BF16), source[:, half:])

    def of_half(x, h):
        return x.reshape(experts, 2, slots, x.shape[-1])[:, h].reshape(rows, x.shape[-1])

    def folded(x):
        x = x.reshape(experts, slots, width)
        return jnp.concatenate([x[:, :, :half], x[:, :, half:]], axis=1)

    def flat(ref):
        return ref[...].reshape(2 * rows, half)

    for copy in loads[:3]:
        copy.wait()
    halves_b, scaled_b, _ = table(routes_b, mix_b)
    scale = jnp.sum(scaled_b, axis=1, keepdims=True)
    send_b[...] = (pick(halves_b, grad) * scale).astype(BF16).reshape(send_b.shape)
    for copy in loads[3:6]:
        copy.wait()
    halves_a, _, weight_a = table(routes_a, mix_a)
    send_a[...] = pick(halves_a, tok).astype(BF16).reshape(send_a.shape)

    pl.semaphore_wait(barrier, experts + groups - 2)
    b_out = exchange(0, send_b, got_b)
    a_out = exchange(1, send_a, got_a)

    for copy in loads[6:9]:
        copy.wait()
    pre = matmul(saved[...], wgu[...])
    gate, up = pre[:, :ff], pre[:, ff:]
    sig = 1.0 / (1.0 + jnp.exp(-gate))
    swish = gate * sig
    act_all[dp] = (swish * up).astype(BF16)
    acts = spread(0, lambda peer: act_all.at[dp], act_all)
    slope = up * sig * (1.0 + gate * (1.0 - sig))
    loads[9].wait()

    for copy in b_out:
        copy.wait_recv()
    wide = flat(got_b).astype(F32)
    for g in range(groups):
        piece = width // groups
        h, at = g * piece // half, g * piece % half
        cols[g] = of_half(wide[:, at:at + piece], h).astype(BF16)
    col_out = spread(1, lambda peer: cols.at[peer], cols_all)
    cols_all[dp] = cols[dp]
    cot = flat(got_b)
    dact = of_half(matmul(cot, wd[:, :half], LAST), 0) + of_half(matmul(cot, wd[:, half:], LAST), 1)
    inner = jnp.concatenate([(dact * slope).astype(BF16), (dact * swish).astype(BF16)], axis=1)
    ret_b[...] = folded(matmul(inner, wgu[...], LAST)).astype(BF16)
    b_back = exchange(2, ret_b, home_b)

    for copy in a_out:
        copy.wait_recv()
    x = flat(got_a)
    pre = of_half(matmul(x, wgu[:half, :]), 0) + of_half(matmul(x, wgu[half:, :]), 1)
    gate, up = pre[:, :ff], pre[:, ff:]
    act = (gate / (1.0 + jnp.exp(-gate)) * up).astype(BF16)
    ret_a[...] = folded(matmul(act, wd[...])).astype(BF16)
    a_back = exchange(3, ret_a, home_a)

    for copy in acts:
        copy.wait_recv()
    for copy in col_out:
        copy.wait_recv()
    step = min(groups, max(1, 256 // rows))

    def term(i):
        left = cols_all[pl.ds(i * step, step)].reshape(step * rows, width // groups)
        return matmul(left, act_all[pl.ds(i * step, step)].reshape(step * rows, ff), FIRST)

    if step == groups:
        out_w[0] = term(0)
    else:
        out_w[0] = lax.fori_loop(1, groups // step, lambda i, total: total + term(i), term(0))

    for copy in b_back:
        copy.wait_recv()
    came = flat(home_b)
    for h in range(2):
        out_b[:, h * half:(h + 1) * half] = matmul(halves_b[h].astype(BF16), came, FIRST).astype(BF16)
    for copy in a_back:
        copy.wait_recv()
    came = flat(home_a)
    for h in range(2):
        mixing = halves_a[h] * weight_a
        high = mixing.astype(BF16)
        low = (mixing - high.astype(F32)).astype(BF16)
        out_a[:, h * half:(h + 1) * half] = (matmul(high, came, FIRST) + matmul(low, came, FIRST)).astype(BF16)

    for copy in (*b_out, *a_out, *acts, *col_out, *b_back, *a_back):
        copy.wait_send()


def on_device(tok, routes_a, mix_a, grad, routes_b, mix_b, saved, gate, up, down):
    experts, groups = lax.axis_size("ep"), lax.axis_size("dp")
    tokens, width = tok.shape
    top = routes_a.shape[1]
    ff = down.shape[1]
    slots = tokens * top // experts
    rows = experts * slots
    piece = width // groups
    block = pltpu.VMEM((experts, 2 * slots, width // 2), BF16)
    table = [pltpu.VMEM((top, tokens), jnp.int32), pltpu.VMEM((top, tokens), F32)]
    return pl.pallas_call(
        functools.partial(kernel, experts, groups, slots),
        out_shape=(
            jax.ShapeDtypeStruct((tokens, width), BF16),
            jax.ShapeDtypeStruct((tokens, width), BF16),
            jax.ShapeDtypeStruct((1, piece, ff), F32),
        ),
        in_specs=[pl.BlockSpec(memory_space=pltpu.MemorySpace.HBM)] * 10,
        out_specs=[pl.BlockSpec(memory_space=pltpu.VMEM)] * 3,
        scratch_shapes=[
            pltpu.VMEM((tokens, width), BF16), *table,
            pltpu.VMEM((tokens, width), BF16), *table,
            pltpu.VMEM((rows, width), BF16),
            pltpu.VMEM((width, 2 * ff), BF16),
            pltpu.VMEM((ff, width), BF16),
            *[block] * 8,
            pltpu.VMEM((groups, rows, piece), BF16),
            pltpu.VMEM((groups, rows, piece), BF16),
            pltpu.VMEM((groups, rows, ff), BF16),
            pltpu.SemaphoreType.DMA((10,)),
            pltpu.SemaphoreType.DMA((4, experts)),
            pltpu.SemaphoreType.DMA((4, experts)),
            pltpu.SemaphoreType.DMA((2, groups)),
            pltpu.SemaphoreType.DMA((2, groups)),
        ],
        compiler_params=pltpu.CompilerParams(collective_id=0, has_side_effects=True, vmem_limit_bytes=40 * 2**20),
    )(tok, routes_a.T, mix_a.T, grad, routes_b.T, mix_b.T, saved, gate, up, down)


def solution(mesh):
    by_token = P(("ep", "dp"), None)
    by_row = P("ep", "dp", None)
    by_expert = P("ep", None, None)
    return jax.shard_map(
        on_device,
        mesh=mesh,
        in_specs=(by_token,) * 6 + (by_row,) + (by_expert,) * 3,
        out_specs=(by_token, by_token, by_row),
        check_vma=False,
    )
```

time: 105 us -> 29.8 us (0.28)
  waiting for transfers between devices: 55 us -> 0 us
  Pallas kernels: 0 us -> 17.2 us
  matrix products: 16.6 us -> 0 us
  starting transfers between devices: 14.8 us -> 0 us
  between operations: 14.2 us -> 0.66 us
  local copies, waits for them, and re-layouts: 1.06 us -> 11.5 us
  other arithmetic: 2.31 us -> 0 us
    reduce_scatter x1 -> x0, waiting for transfers between devices: 44.9 us -> none  [on_device(): lax.psum_scatter(weight_terms(cot_all, hidden_all), 'dp', scatter_dimensi...]
    pallas_call x0 -> x1, Pallas kernels: none -> 17.2 us  [on_device(): pl.pallas_call(functools.partial(kernel, experts, groups, slots), out_sha...]
    dot_general x12 -> x0, matrix products: 16.6 us -> none  [the longest x1 2.84 us: expert_forward(): jnp.dot(hidden, w_down[0], preferred_element_type=jnp.float32)]
    all_to_all x4 -> x0, starting transfers between devices: 14.8 us -> none  [the longest x1 4.24 us: on_device(): lax.all_to_all(send_grads, 'ep', split_axis=0, concat_axis=0, tiled=True)]
    unnamed x30 -> x23, local copies, waits for them, and re-layouts: 0.72 us -> 11.5 us
    all_to_all x4 -> x0, waiting for transfers between devices: 9.98 us -> none  [the longest x1 4 us: on_device(): lax.all_to_all(send_tokens, 'ep', split_axis=0, concat_axis=0, tiled=True)]
    reduce_sum x5 -> x0, other arithmetic: 2.22 us -> none  [the longest x2 1.3 us: slot_tables(): mixing = jnp.sum(jnp.where(hits, weights[:, :, None], 0.0), axis=1)]
  transfers between devices with their start and end apart: 5 -> 0, of which waited for: 5 -> 0; matrix products, arithmetic and copies ran while one was open for 13% -> 0% of each run, Pallas kernels for 0% -> 0%
where the time goes in v1:
time: 29.8 us; the launch traced here: 29.4 us
  Pallas kernels  17.2 us (58%)
  local copies, waits for them, and re-layouts  11.5 us (39%)
  between operations  0.66 us (2%)
    pallas_call x1, Pallas kernels, on_device(): pl.pallas_call(functools.partial(kernel, experts, groups, slots), out_sha...  17.2 us
    unnamed x23, local copies, waits for them, and re-layouts  11.5 us

profile of v1, /device:TPU:0, one launch (start us, length us, event | category | flops | bytes accessed | tf_op | source)
XLA Modules:
  0.0 29.4 jit_solution(5252721574646736212)
XLA Ops:
  0.6 0.0 copy-start
  0.6 1.4 %copy-done = bf16[1,2048,384]{2,1,0:T(8,128)(2,1)S(1)} copy-done((bf16[1,2048,384]{2,1,0:T(8,128)(2,1)S(1)}, bf16[1,2048,384]{2,1,0:T(8,128)(2,1)}, u32[]{:S(2)}) %copy-start) | copy-done | bytes 1572888
  2.0 0.0 copy-start.1
  2.0 1.4 %copy-done.1 = bf16[1,2048,384]{2,1,0:T(8,128)(2,1)S(1)} copy-done((bf16[1,2048,384]{2,1,0:T(8,128)(2,1)S(1)}, bf16[1,2048,384]{2,1,0:T(8,128)(2,1)}, u32[]{:S(2)}) %copy-start.1) | copy-done | bytes 1572888
  3.5 0.0 copy-start.2
  3.5 1.4 %copy-done.2 = bf16[1,384,2048]{2,1,0:T(8,128)(2,1)S(1)} copy-done((bf16[1,384,2048]{2,1,0:T(8,128)(2,1)S(1)}, bf16[1,384,2048]{2,1,0:T(8,128)(2,1)}, u32[]{:S(2)}) %copy-start.2) | copy-done | bytes 1572888
  4.9 0.0 copy-start.3
  4.9 0.9 %copy-done.3 = bf16[1,32,2048]{2,1,0:T(8,128)(2,1)S(1)} copy-done((bf16[1,32,2048]{2,1,0:T(8,128)(2,1)S(1)}, bf16[1,32,2048]{2,1,0:T(8,128)(2,1)}, u32[]{:S(2)}) %copy-start.3) | copy-done | bytes 131096
  5.8 0.0 copy-start.4
  5.8 0.8 %copy-done.4 = bf16[16,2048]{1,0:T(8,128)(2,1)S(1)} copy-done((bf16[16,2048]{1,0:T(8,128)(2,1)S(1)}, bf16[16,2048]{1,0:T(8,128)(2,1)}, u32[]{:S(2)}) %copy-start.4) | copy-done | bytes 65560
  6.6 0.0 copy-start.5
  6.6 0.8 %copy-done.5 = bf16[16,2048]{1,0:T(8,128)(2,1)S(1)} copy-done((bf16[16,2048]{1,0:T(8,128)(2,1)S(1)}, bf16[16,2048]{1,0:T(8,128)(2,1)}, u32[]{:S(2)}) %copy-start.5) | copy-done | bytes 65560
  7.4 0.0 copy-start.6
  7.4 0.7 %copy-done.6 = s32[16,2]{0,1:T(2,128)S(1)} copy-done((s32[16,2]{0,1:T(2,128)S(1)}, s32[16,2]{0,1:T(2,128)}, u32[]{:S(2)}) %copy-start.6) | copy-done | bytes 152
  8.1 0.0 copy-start.7
  8.1 0.7 %copy-done.7 = f32[16,2]{0,1:T(2,128)S(1)} copy-done((f32[16,2]{0,1:T(2,128)S(1)}, f32[16,2]{0,1:T(2,128)}, u32[]{:S(2)}) %copy-start.7) | copy-done | bytes 152
  8.8 0.0 copy-start.8
  8.8 0.7 %copy-done.8 = s32[16,2]{0,1:T(2,128)S(1)} copy-done((s32[16,2]{0,1:T(2,128)S(1)}, s32[16,2]{0,1:T(2,128)}, u32[]{:S(2)}) %copy-start.8) | copy-done | bytes 152
  9.5 0.0 copy-start.9
  9.5 0.7 %copy-done.9 = f32[16,2]{0,1:T(2,128)S(1)} copy-done((f32[16,2]{0,1:T(2,128)S(1)}, f32[16,2]{0,1:T(2,128)}, u32[]{:S(2)}) %copy-start.9) | copy-done | bytes 152
  10.2 17.2 %shard_map.121 = (bf16[16,2048]{1,0:T(8,128)(2,1)S(1)}, bf16[16,2048]{1,0:T(8,128)(2,1)S(1)}, f32[1,256,384]{2,1,0:T(8,128)S(1)}) custom-call(bf16[16,2048]{1,0:T(8,128)(2,1)S(1)} %copy-done.4, s32[2,16]{1,0:T(2,128)S(1)} %bitcast.4, f32[2,16]{1,0:T(2,128)S(1)} %bitcast.5, bf16[16,2048]{1,0:T(8,128)(2,1)S(1)} %copy-done.5, s32[2,16]{1,0:T(2,128)S(1)} %bitcast.6, ...), custom_call_target="tpu_custom_call" | custom-call | tf_op jit(solution)/shard_map/pallas_call | solution.py:201
  27.4 0.6 %copy.16 = bf16[16,2048]{1,0:T(8,128)(2,1)} copy(bf16[16,2048]{1,0:T(8,128)(2,1)S(1)} %get-tuple-element.6) | data formatting | bytes 131072
  28.0 0.6 %copy.17 = bf16[16,2048]{1,0:T(8,128)(2,1)} copy(bf16[16,2048]{1,0:T(8,128)(2,1)S(1)} %get-tuple-element.7) | data formatting | bytes 131072
  28.6 0.7 %copy.18 = f32[1,256,384]{2,1,0:T(8,128)} copy(f32[1,256,384]{2,1,0:T(8,128)S(1)} %get-tuple-element.8) | data formatting | bytes 786432
Async XLA Ops:
  0.6 1.4 %copy-start = (bf16[1,2048,384]{2,1,0:T(8,128)(2,1)S(1)}, bf16[1,2048,384]{2,1,0:T(8,128)(2,1)}, u32[]{:S(2)}) copy-start(bf16[1,2048,384]{2,1,0:T(8,128)(2,1)} %gate_hbm.1) | copy-start | bytes 4718596
  2.0 1.4 %copy-start.1 = (bf16[1,2048,384]{2,1,0:T(8,128)(2,1)S(1)}, bf16[1,2048,384]{2,1,0:T(8,128)(2,1)}, u32[]{:S(2)}) copy-start(bf16[1,2048,384]{2,1,0:T(8,128)(2,1)} %up_hbm.1) | copy-start | bytes 4718596
  3.5 1.4 %copy-start.2 = (bf16[1,384,2048]{2,1,0:T(8,128)(2,1)S(1)}, bf16[1,384,2048]{2,1,0:T(8,128)(2,1)}, u32[]{:S(2)}) copy-start(bf16[1,384,2048]{2,1,0:T(8,128)(2,1)} %down_hbm.1) | copy-start | bytes 4718596
  4.9 0.9 %copy-start.3 = (bf16[1,32,2048]{2,1,0:T(8,128)(2,1)S(1)}, bf16[1,32,2048]{2,1,0:T(8,128)(2,1)}, u32[]{:S(2)}) copy-start(bf16[1,32,2048]{2,1,0:T(8,128)(2,1)} %saved_hbm.1) | copy-start | bytes 393220
  5.8 0.8 %copy-start.4 = (bf16[16,2048]{1,0:T(8,128)(2,1)S(1)}, bf16[16,2048]{1,0:T(8,128)(2,1)}, u32[]{:S(2)}) copy-start(bf16[16,2048]{1,0:T(8,128)(2,1)} %tok_hbm.1) | copy-start | bytes 196612
  6.6 0.8 %copy-start.5 = (bf16[16,2048]{1,0:T(8,128)(2,1)S(1)}, bf16[16,2048]{1,0:T(8,128)(2,1)}, u32[]{:S(2)}) copy-start(bf16[16,2048]{1,0:T(8,128)(2,1)} %grad_hbm.1) | copy-start | bytes 196612
  7.4 0.7 %copy-start.6 = (s32[16,2]{0,1:T(2,128)S(1)}, s32[16,2]{0,1:T(2,128)}, u32[]{:S(2)}) copy-start(s32[16,2]{0,1:T(2,128)} %param.11) | copy-start | bytes 388
  8.1 0.7 %copy-start.7 = (f32[16,2]{0,1:T(2,128)S(1)}, f32[16,2]{0,1:T(2,128)}, u32[]{:S(2)}) copy-start(f32[16,2]{0,1:T(2,128)} %param.12) | copy-start | bytes 388
  8.8 0.7 %copy-start.8 = (s32[16,2]{0,1:T(2,128)S(1)}, s32[16,2]{0,1:T(2,128)}, u32[]{:S(2)}) copy-start(s32[16,2]{0,1:T(2,128)} %param.14) | copy-start | bytes 388
  9.5 0.7 %copy-start.9 = (f32[16,2]{0,1:T(2,128)S(1)}, f32[16,2]{0,1:T(2,128)}, u32[]{:S(2)}) copy-start(f32[16,2]{0,1:T(2,128)} %param.15) | copy-start | bytes 388

commit v2 on v1

--- a/solution.py
+++ b/solution.py
@@ -188,6 +188,15 @@
         copy.wait_send()
 
 
+def store(*refs):
+    sems = refs[6]
+    copies = [pltpu.make_async_copy(refs[i], refs[3 + i], sems.at[i]) for i in range(3)]
+    for copy in copies:
+        copy.start()
+    for copy in copies:
+        copy.wait()
+
+
 def on_device(tok, routes_a, mix_a, grad, routes_b, mix_b, saved, gate, up, down):
     experts, groups = lax.axis_size("ep"), lax.axis_size("dp")
     tokens, width = tok.shape
@@ -198,7 +207,7 @@
     piece = width // groups
     block = pltpu.VMEM((experts, 2 * slots, width // 2), BF16)
     table = [pltpu.VMEM((top, tokens), jnp.int32), pltpu.VMEM((top, tokens), F32)]
-    return pl.pallas_call(
+    outs = pl.pallas_call(
         functools.partial(kernel, experts, groups, slots),
         out_shape=(
             jax.ShapeDtypeStruct((tokens, width), BF16),
@@ -224,7 +233,18 @@
             pltpu.SemaphoreType.DMA((2, groups)),
         ],
         compiler_params=pltpu.CompilerParams(collective_id=0, has_side_effects=True, vmem_limit_bytes=40 * 2**20),
-    )(tok, routes_a.T, mix_a.T, grad, routes_b.T, mix_b.T, saved, gate, up, down)
+    )(*[
+        pltpu.with_memory_space_constraint(x, pltpu.MemorySpace.HBM)
+        for x in (tok, routes_a.T, mix_a.T, grad, routes_b.T, mix_b.T, saved, gate, up, down)
+    ])
+    return pl.pallas_call(
+        store,
+        out_shape=tuple(jax.ShapeDtypeStruct(x.shape, x.dtype) for x in outs),
+        in_specs=[pl.BlockSpec(memory_space=pl.ANY)] * 3,
+        out_specs=[pl.BlockSpec(memory_space=pl.ANY)] * 3,
+        scratch_shapes=[pltpu.SemaphoreType.DMA((3,))],
+        compiler_params=pltpu.CompilerParams(vmem_limit_bytes=2**20),
+    )(*outs)
 
 
 def solution(mesh):

time: 29.8 us -> 18.1 us (0.61)
  local copies, waits for them, and re-layouts: 11.5 us -> 0 us
    unnamed x23 -> x0, local copies, waits for them, and re-layouts: 11.5 us -> none
    pallas_call x0 -> x1, Pallas kernels: none -> 0.82 us  [on_device(): pl.pallas_call(store, out_shape=tuple((jax.ShapeDtypeStruct(x.shape, x.dt...]
    pallas_call x1, Pallas kernels: 17.2 us -> 16.5 us  [on_device(): pl.pallas_call(functools.partial(kernel, experts, groups, slots), out_sha...]
where the time goes in v2:
time: 18.1 us; the launch traced here: 18 us
  Pallas kernels  17.3 us (96%)
  between operations  0.64 us (4%)
    pallas_call x1, Pallas kernels, on_device(): pl.pallas_call(functools.partial(kernel, experts, groups, slots), out_sha...  16.5 us
    pallas_call x1, Pallas kernels, on_device(): pl.pallas_call(store, out_shape=tuple((jax.ShapeDtypeStruct(x.shape, x.dt...  0.82 us

profile of v2, /device:TPU:0, one launch (start us, length us, event | category | flops | bytes accessed | tf_op | source)
XLA Modules:
  0.0 18.0 jit_solution(8095149161971070693)
XLA Ops:
  0.6 16.5 %shard_map.121 = (bf16[16,2048]{1,0:T(8,128)(2,1)S(1)}, bf16[16,2048]{1,0:T(8,128)(2,1)S(1)}, f32[1,256,384]{2,1,0:T(8,128)S(1)}) custom-call(bf16[16,2048]{1,0:T(8,128)(2,1)} %tok_hbm.1, s32[2,16]{1,0:T(2,128)} %bitcast.4, f32[2,16]{1,0:T(2,128)} %bitcast.5, bf16[16,2048]{1,0:T(8,128)(2,1)} %grad_hbm.1, s32[2,16]{1,0:T(2,128)} %bitcast.6, f32[2,16]{1,0:T(2,128)} %bitcast.7, ...), custom_call_target="tpu_custom_call" | custom-call | tf_op jit(solution)/shard_map/pallas_call | solution.py:210
  17.2 0.8 %shard_map.122 = (bf16[16,2048]{1,0:T(8,128)(2,1)}, bf16[16,2048]{1,0:T(8,128)(2,1)}, f32[1,256,384]{2,1,0:T(8,128)}) custom-call(bf16[16,2048]{1,0:T(8,128)(2,1)S(1)} %get-tuple-element.6.refs_0_, bf16[16,2048]{1,0:T(8,128)(2,1)S(1)} %get-tuple-element.7.refs_1_, f32[1,256,384]{2,1,0:T(8,128)S(1)} %get-tuple-element.8.refs_2_), custom_call_target="tpu_custom_call" | custom-call | tf_op jit(solution)/shard_map/pallas_call | solution.py:240

commit v3 on v2

--- a/solution.py
+++ b/solution.py
@@ -35,7 +35,10 @@
         (routes_b_hbm, routes_b), (mix_b_hbm, mix_b), (grad_hbm, grad),
         (routes_a_hbm, routes_a), (mix_a_hbm, mix_a), (tok_hbm, tok),
         (saved_hbm.at[0], saved),
-        (gate_hbm.at[0], wgu.at[:, pl.ds(0, ff)]), (up_hbm.at[0], wgu.at[:, pl.ds(ff, ff)]),
+        *(
+            (src.at[0, pl.ds(h * half, half)], wgu.at[pl.ds(h * half, half), pl.ds(at, ff)])
+            for h in range(2) for src, at in ((gate_hbm, 0), (up_hbm, ff))
+        ),
         (down_hbm.at[0], wd),
     ):
         copy = pltpu.make_async_copy(src, dst, load_sem.at[len(loads)])
@@ -106,13 +109,11 @@
     def flat(ref):
         return ref[...].reshape(2 * rows, half)
 
-    for copy in loads[:3]:
+    for copy in loads[:6]:
         copy.wait()
     halves_b, scaled_b, _ = table(routes_b, mix_b)
     scale = jnp.sum(scaled_b, axis=1, keepdims=True)
     send_b[...] = (pick(halves_b, grad) * scale).astype(BF16).reshape(send_b.shape)
-    for copy in loads[3:6]:
-        copy.wait()
     halves_a, _, weight_a = table(routes_a, mix_a)
     send_a[...] = pick(halves_a, tok).astype(BF16).reshape(send_a.shape)
 
@@ -122,14 +123,17 @@
 
     for copy in loads[6:9]:
         copy.wait()
-    pre = matmul(saved[...], wgu[...])
+    pre = matmul(saved[:, :half], wgu[:half, :])
+    for copy in loads[9:11]:
+        copy.wait()
+    pre = pre + matmul(saved[:, half:], wgu[half:, :])
     gate, up = pre[:, :ff], pre[:, ff:]
     sig = 1.0 / (1.0 + jnp.exp(-gate))
     swish = gate * sig
     act_all[dp] = (swish * up).astype(BF16)
     acts = spread(0, lambda peer: act_all.at[dp], act_all)
     slope = up * sig * (1.0 + gate * (1.0 - sig))
-    loads[9].wait()
+    loads[11].wait()
 
     for copy in b_out:
         copy.wait_recv()
@@ -142,8 +146,8 @@
     cols_all[dp] = cols[dp]
     cot = flat(got_b)
     dact = of_half(matmul(cot, wd[:, :half], LAST), 0) + of_half(matmul(cot, wd[:, half:], LAST), 1)
-    inner = jnp.concatenate([(dact * slope).astype(BF16), (dact * swish).astype(BF16)], axis=1)
-    ret_b[...] = folded(matmul(inner, wgu[...], LAST)).astype(BF16)
+    both = jnp.concatenate([(dact * slope).astype(BF16), (dact * swish).astype(BF16)], axis=1)
+    ret_b[...] = folded(matmul(both, wgu[...], LAST)).astype(BF16)
     b_back = exchange(2, ret_b, home_b)
 
     for copy in a_out:
@@ -226,7 +230,7 @@
             pltpu.VMEM((groups, rows, piece), BF16),
             pltpu.VMEM((groups, rows, piece), BF16),
             pltpu.VMEM((groups, rows, ff), BF16),
-            pltpu.SemaphoreType.DMA((10,)),
+            pltpu.SemaphoreType.DMA((12,)),
             pltpu.SemaphoreType.DMA((4, experts)),
             pltpu.SemaphoreType.DMA((4, experts)),
             pltpu.SemaphoreType.DMA((2, groups)),

time: 18.1 us -> 18.1 us (level)
  no operation moved by 1% of the time
where the time goes in v3:
time: 18.1 us; the launch traced here: 18 us
  Pallas kernels  17.4 us (96%)
  between operations  0.64 us (4%)
    pallas_call x1, Pallas kernels, on_device(): pl.pallas_call(functools.partial(kernel, experts, groups, slots), out_sha...  16.5 us
    pallas_call x1, Pallas kernels, on_device(): pl.pallas_call(store, out_shape=tuple((jax.ShapeDtypeStruct(x.shape, x.dt...  0.82 us

profile of v3, /device:TPU:0, one launch (start us, length us, event | category | flops | bytes accessed | tf_op | source)
XLA Modules:
  0.0 18.0 jit_solution(14298518105567021088)
XLA Ops:
  0.6 16.5 %shard_map.121 = (bf16[16,2048]{1,0:T(8,128)(2,1)S(1)}, bf16[16,2048]{1,0:T(8,128)(2,1)S(1)}, f32[1,256,384]{2,1,0:T(8,128)S(1)}) custom-call(bf16[16,2048]{1,0:T(8,128)(2,1)} %tok_hbm.1, s32[2,16]{1,0:T(2,128)} %bitcast.4, f32[2,16]{1,0:T(2,128)} %bitcast.5, bf16[16,2048]{1,0:T(8,128)(2,1)} %grad_hbm.1, s32[2,16]{1,0:T(2,128)} %bitcast.6, f32[2,16]{1,0:T(2,128)} %bitcast.7, ...), custom_call_target="tpu_custom_call" | custom-call | tf_op jit(solution)/shard_map/pallas_call | solution.py:214
  17.2 0.8 %shard_map.122 = (bf16[16,2048]{1,0:T(8,128)(2,1)}, bf16[16,2048]{1,0:T(8,128)(2,1)}, f32[1,256,384]{2,1,0:T(8,128)}) custom-call(bf16[16,2048]{1,0:T(8,128)(2,1)S(1)} %get-tuple-element.6.refs_0_, bf16[16,2048]{1,0:T(8,128)(2,1)S(1)} %get-tuple-element.7.refs_1_, f32[1,256,384]{2,1,0:T(8,128)S(1)} %get-tuple-element.8.refs_2_), custom_call_target="tpu_custom_call" | custom-call | tf_op jit(solution)/shard_map/pallas_call | solution.py:244
